TPU v7x, 32 devices: a whole 2x2x4 slice. The times are simulated.
32 devices in a mesh: rep: 2 (over x), head: 8 (over z, y), req: 2 (over core).
Axes of the slice: x: 2, y: 2, z: 4, core: 2. Of those that a mesh axis runs over, the one named last changes fastest.
Arguments:
- hidden: bfloat16 [8, 512, 8192], P(('rep', 'req'), None, 'head'), parts along dimension 0, may hold values from -6 to 6
- lengths: int32 [8], P(('rep', 'req')), parts along dimension 0, may hold values from 128 to 512, as said below
- hit_slots: int32 [8], P('rep'), parts along dimension 0, may hold values from -1 to 15, as said below
- placement: int32 [8], P('rep'), parts along dimension 0, may hold values from 0 to 3, as said below
- state_pool: bfloat16 [32, 128, 64, 128], P(('rep', 'req'), 'head'), parts along dimension 0, may hold values from -3 to 3
- in_weight: bfloat16 [8192, 16512], P('req', 'head'), may hold values from -0.0625 to 0.0625
- group_weight: bfloat16 [8192, 1024], P('req', 'head'), may hold values from -0.0625 to 0.0625
- out_weight: bfloat16 [8192, 8192], P('head'), may hold values from -0.0625 to 0.0625
- decay_rate: float32 [128], P('head'), may hold values from 0.02 to 2
- step_bias: float32 [128], P('head'), may hold values from -4.6 to -3.2
- skip_gain: float32 [128], P('head'), may hold values from 0.5 to 1.5
Outputs:
- mixed: bfloat16 [8, 512, 8192], P(('rep', 'req'), None, 'head'), parts along dimension 0
- decode_states: bfloat16 [8, 128, 64, 128], P(('rep', 'req'), 'head'), parts along dimension 0
There are 2 independent parts, one for each index of `rep`. A program takes and returns all parts, laid end to end along the dimension named above; an argument that names none is the same for every part. Nothing has to cross between parts.
Inputs may be any that keep to these rules, and one draw needn't show every extreme that they name: `lengths`: every live length lies in 128 .. 512 and one request of each part has 512. `hit_slots`: -1 marks a miss; slot s lives on req index s // 8; requests may share a slot. `placement`: a permutation of the requests; decode slot s lives on req index s // 2.
All inputs are finite; a program needn't handle non-finite values.
Results may differ from a plain program's by a relative error of at most 0.0076.
Values may be sent and summed in bfloat16 or wider, within the bound.
A program may use at most 256 MiB of HBM per device.

v0:
```python
import jax
import jax.numpy as jnp
from jax import lax
from jax.sharding import PartitionSpec as P

P_SIZE = 64
N = 128
G = 4
Q = 256


precise = lax.Precision.HIGHEST


def from_partner(value, axis, bit):
    mask = 2**bit
    pairs = [(source, source ^ mask) for source in range(lax.axis_size(axis))]
    return lax.ppermute(value, axis, pairs)


def span_scan(inputs, step_sizes, b_heads, c_heads, decay_rates, initial):
    requests, length, head_count, head_width = inputs.shape
    state_size = b_heads.shape[-1]
    spans = length // Q
    x_span = inputs.reshape(requests, spans, Q, head_count, head_width)
    dt_span = step_sizes.reshape(requests, spans, Q, head_count)
    b_span = b_heads.reshape(requests, spans, Q, head_count, state_size)
    c_span = c_heads.reshape(requests, spans, Q, head_count, state_size)
    log_decay = jnp.cumsum(-dt_span * decay_rates, axis=2)
    within = jnp.arange(Q)[:, None] >= jnp.arange(Q)[None, :]
    spread = log_decay[:, :, :, None, :] - log_decay[:, :, None, :, :]
    decays = jnp.exp(jnp.where(within[None, None, :, :, None], spread, -jnp.inf))
    scores = jnp.einsum("bctkn,bcskn->bctsk", c_span, b_span, precision=precise)
    mixing = scores * decays * dt_span[:, :, None, :, :]
    intra_out = jnp.einsum("bctsk,bcskp->bctkp", mixing, x_span, precision=precise)
    to_end = jnp.exp(log_decay[:, :, -1:, :] - log_decay) * dt_span
    span_states = jnp.einsum(
        "bcskp,bcskn->bckpn", x_span * to_end[..., None], b_span, precision=precise
    )
    through = jnp.exp(log_decay[:, :, -1, :])
    running = initial
    entering = []
    for span_index in range(spans):
        entering.append(running)
        running = through[:, span_index, :, None, None] * running + span_states[:, span_index]
    entering = jnp.stack(entering, axis=1)
    carried = jnp.exp(log_decay)[..., None] * jnp.einsum(
        "bctkn,bckpn->bctkp", c_span, entering, precision=precise
    )
    return ((intra_out + carried).reshape(requests, length, head_count, head_width), running)


def fetch_states(hit_slots, state_pool, local_requests):
    slot_count = state_pool.shape[0]
    local_slot = hit_slots - lax.axis_index("req") * slot_count
    selector = (local_slot[:, None] == jnp.arange(slot_count)[None, :]).astype(jnp.bfloat16)
    outgoing = jnp.dot(
        selector, state_pool.reshape(slot_count, -1), preferred_element_type=jnp.float32
    )
    outgoing = outgoing.astype(jnp.bfloat16).reshape((hit_slots.shape[0],) + state_pool.shape[1:])
    incoming = lax.all_to_all(outgoing, "req", split_axis=0, concat_axis=0, tiled=True)
    incoming = incoming.reshape((lax.axis_size("req"), local_requests) + state_pool.shape[1:])
    return jnp.sum(incoming.astype(jnp.float32), axis=0)


def body(
    hidden,
    lengths,
    hit_slots,
    placement,
    state_pool,
    in_weight,
    group_weight,
    out_weight,
    decay_rate,
    step_bias,
    skip_gain,
):
    local_requests, length, feature_piece = hidden.shape
    head_count = decay_rate.shape[0]
    token_rows = local_requests * length
    column_count = in_weight.shape[1]
    per_head = column_count // head_count
    flat_tokens = hidden.reshape(token_rows, feature_piece)
    whole_rows = lax.all_gather(flat_tokens, "head", axis=1, tiled=True)
    half_rows = lax.all_to_all(whole_rows, "req", split_axis=1, concat_axis=0, tiled=True)
    head_part = jnp.dot(half_rows, in_weight, preferred_element_type=jnp.float32)
    group_part = jnp.dot(half_rows, group_weight, preferred_element_type=jnp.float32)
    summed = lax.psum_scatter(
        jnp.concatenate([head_part, group_part], axis=1), "req", scatter_dimension=0, tiled=True
    )
    projected = summed[:, :column_count]
    group_sum = summed[:, column_count:]
    projected = projected.reshape(local_requests, length, head_count, per_head)
    inputs = projected[..., :P_SIZE].astype(jnp.bfloat16)
    gate_in = projected[..., P_SIZE : 2 * P_SIZE].astype(jnp.bfloat16)
    step_raw = projected[..., 2 * P_SIZE]
    group_piece = group_sum.astype(jnp.bfloat16)
    group_devices = lax.axis_size("head") // G
    position = lax.axis_index("head") % group_devices
    for bit in range(group_devices.bit_length() - 1):
        partner = from_partner(group_piece, "head", bit)
        upper = position // (1 << bit) % 2 == 1
        group_piece = jnp.where(
            upper,
            jnp.concatenate([partner, group_piece], axis=1),
            jnp.concatenate([group_piece, partner], axis=1),
        )
    group_in = group_piece.reshape(local_requests, length, 2 * N)
    b_group = group_in[..., :N].astype(jnp.float32)
    c_group = group_in[..., N:].astype(jnp.float32)
    b_heads = jnp.broadcast_to(b_group[:, :, None, :], (local_requests, length, head_count, N))
    c_heads = jnp.broadcast_to(c_group[:, :, None, :], (local_requests, length, head_count, N))
    live_mask = jnp.arange(length)[None, :] < lengths[:, None]
    step_sizes = jnp.where(live_mask[..., None], jax.nn.softplus(step_raw + step_bias), 0.0)
    inputs_f = inputs.astype(jnp.float32)
    initial = fetch_states(hit_slots, state_pool, local_requests)
    scanned, finals = span_scan(inputs_f, step_sizes, b_heads, c_heads, decay_rate, initial)
    outputs = scanned + skip_gain[:, None] * inputs_f
    gated = jnp.where(
        live_mask[..., None, None], outputs * jax.nn.silu(gate_in.astype(jnp.float32)), 0.0
    )
    gated = gated.astype(jnp.bfloat16).reshape(token_rows, head_count * P_SIZE)
    mixed_cols = lax.psum_scatter(
        lax.dot_general(
            out_weight, gated, (((0,), (1,)), ((), ())), preferred_element_type=jnp.float32
        ),
        "head",
        scatter_dimension=0,
        tiled=True,
    )
    mixed = mixed_cols.T.astype(jnp.bfloat16).reshape(local_requests, length, feature_piece)
    request_total = placement.shape[0]
    my_targets = lax.dynamic_slice_in_dim(
        placement, lax.axis_index("req") * local_requests, local_requests, 0
    )
    router = (jnp.arange(request_total)[:, None] == my_targets[None, :]).astype(jnp.bfloat16)
    leaving = jnp.dot(
        router,
        finals.astype(jnp.bfloat16).reshape(local_requests, -1),
        preferred_element_type=jnp.float32,
    )
    leaving = leaving.astype(jnp.bfloat16).reshape(request_total, head_count, P_SIZE, N)
    arrived = lax.all_to_all(leaving, "req", split_axis=0, concat_axis=0, tiled=True)
    arrived = arrived.reshape(lax.axis_size("req"), local_requests, head_count, P_SIZE, N).astype(
        jnp.float32
    )
    decode_states = jnp.sum(arrived, axis=0).astype(jnp.bfloat16)
    return (mixed, decode_states)


def solution(mesh):
    in_specs = (
        P(("rep", "req"), None, "head"),
        P(("rep", "req")),
        P("rep"),
        P("rep"),
        P(("rep", "req"), "head", None, None),
        P("req", "head"),
        P("req", "head"),
        P("head", None),
        P("head"),
        P("head"),
        P("head"),
    )
    out_specs = (P(("rep", "req"), None, "head"), P(("rep", "req"), "head", None, None))
    return jax.shard_map(body, mesh=mesh, in_specs=in_specs, out_specs=out_specs, check_vma=False)
```

profile of v0, /device:TPU:0, one launch (start us, length us, event | category | flops | bytes accessed | tf_op | source)
XLA Modules:
  0.0 1075.9 jit_solution(5051242135348496677)
XLA Ops:
  7.2 0.0 all-gather.2.cloned.1.call-start
  7.2 4.0 copy.88
  11.3 0.0 reduce-scatter.3.cloned.1.call-start
  11.3 230.4 %all-gather.2.cloned.1.call-done = bf16[1024,8192]{0,1:T(8,128)(2,1)} async-done(((bf16[1024,1024]{0,1:T(8,128)(2,1)}), bf16[1024,8192]{0,1:T(8,128)(2,1)}) %all-gather.2.cloned.1.call-update) | async-done | bytes 16777232 | tf_op jit(solution)/shard_map/all_gather | solution.py:85
  241.7 31.5 %all_to_all.29 = bf16[1024,2,4096]{0,2,1:T(8,128)(2,1)} all-to-all(bf16[1024,2,4096]{0,2,1:T(8,128)(2,1)} %bitcast.131), channel_id=1, replica_groups=mesh['rep'=2,'head'=8,'req'=2] {'req'}, dimensions={1} | all-to-all | bytes 33554432 | tf_op jit(solution)/shard_map/all_to_all | solution.py:86
  273.3 21.0 %copy.73 = bf16[2,1024,4096]{2,1,0:T(8,128)(2,1)} copy(bf16[2,1024,4096]{1,2,0:T(8,128)(2,1)} %bitcast.128) | data formatting | bytes 33554432 | tf_op jit(solution)/shard_map/all_to_all | solution.py:86
  294.3 11.4 %fusion.54 = f32[2048,128]{0,1:T(8,128)S(1)} fusion(bf16[2048,4096]{1,0:T(8,128)(2,1)} %bitcast.126, bf16[4096,128]{1,0:T(8,128)(2,1)S(1)} %copy-done), kind=kOutput, calls=%fused_computation.83 | convolution fusion | flops 2147483648 | bytes 18874368 | tf_op jit(solution)/shard_map/dot_general | solution.py:88
  305.7 45.6 %fusion.53 = f32[2048,2064]{0,1:T(8,128)} fusion(bf16[2048,4096]{1,0:T(8,128)(2,1)} %bitcast.127, bf16[4096,2064]{0,1:T(8,128)(2,1)} %param.16), kind=kOutput, calls=%fused_computation.82 | convolution fusion | flops 34628173824 | bytes 50593792 | tf_op jit(solution)/shard_map/dot_general | solution.py:87
  351.3 11.9 %pad_maximum_fusion = f32[2048,2192]{0,1:T(8,128)} fusion(f32[2048,128]{0,1:T(8,128)S(1)} %fusion.54, f32[2048,2064]{0,1:T(8,128)} %fusion.53), kind=kLoop, calls=%fused_computation.2 | loop fusion | flops 4489216 | bytes 35913728 | tf_op jit(solution)/shard_map/concatenate | solution.py:90
  363.2 0.0 reduce-scatter.3.cloned.1.call-update
  363.2 0.6 copy-done.8
  363.9 0.9 copy-done.2
  364.8 1.4 fusion.36
  366.3 1.1 copy.99
  367.4 3.8 all-to-all-start.1
  371.2 0.2 reduce-scatter.5.cloned.1.call-start
  371.5 2.2 all-to-all-done.1
  373.7 0.2 convert_reduce_fusion
  373.9 0.1 iota_compare_fusion.1
  374.0 0.1 broadcast_compare_fusion
  374.0 15.3 %reduce-scatter.3.cloned.1.call-done = f32[1024,2192]{0,1:T(8,128)} async-done(((f32[2048,2192]{0,1:T(8,128)}), f32[1024,2192]{0,1:T(8,128)}) %reduce-scatter.3.cloned.1.call-update) | async-done | bytes 8978448 | tf_op jit(solution)/shard_map/reduce_scatter | solution.py:89
  389.3 8.3 slice.60
  397.6 11.9 %reshape.168 = f32[2,512,16,129]{1,0,3,2:T(2,128)} reshape(f32[1024,2064]{0,1:T(8,128)} %slice.60) | data formatting | bytes 16908288 | tf_op jit(solution)/shard_map/reshape | solution.py:94
  409.6 6.8 copy.136
  416.4 0.1 reshape.183
  416.5 0.1 multiply_bitcast_fusion
  416.6 2.3 reduce-window.6
  418.9 0.2 slice_reduce_fusion
  419.1 0.1 bitcast_bitcast_fusion
  419.2 0.2 slice_reduce_fusion.1
  419.4 0.1 fusion.48
  419.5 0.1 copy.83
  419.6 1.1 slice.83
  420.6 2.2 collective-permute-start
  422.8 5.1 fusion.50
  427.9 5.9 reshape.174
  433.8 7.0 broadcast_multiply_fusion
  440.7 0.2 concatenate.17
  440.9 0.2 concatenate.16
  441.1 1.2 broadcast_select_fusion
  442.3 0.4 slice_convert_fusion.2
  442.6 0.2 copy.89
  442.9 0.2 copy.90
  443.1 6.1 fusion.18
  449.3 14.0 %fusion.22 = f32[2,2,16,256,256]{4,3,2,1,0:T(8,128)S(1)} fusion(f32[2,2,256,128]{3,2,1,0:T(8,128)S(1)} %bitcast.135, f32[2,2,256,128]{3,2,1,0:T(8,128)S(1)} %bitcast.138), kind=kOutput, calls=%fused_computation.30 | convolution fusion | flops 6442450944 | bytes 17825792 | tf_op jit(solution)/shard_map/bctkn,bcskn->bctsk/dot_general | solution.py:33
  463.2 1.3 fusion.51
  464.5 10.1 fusion.20
  474.6 12.9 %fusion.17 = f32[2,2,16,8,8,256]{5,4,3,2,1,0:T(8,128)S(1)} fusion(f32[2,2,16,64,256]{4,3,2,1,0:T(8,128)} %fusion.20, f32[2,2,16,256,256]{4,3,2,1,0:T(8,128)S(1)} %fusion.22, f32[2,2,256,16]{2,3,1,0:T(8,128)S(1)} %get-tuple-element.3, f32[2,2,256,16]{2,3,1,0:T(8,128)S(1)} %bitcast_bitcast_fusion, pred[256,256]{0,1:T(8,128)(4,1)S(1)} %iota_compare_fusion, ...), kind=kOutput, calls=%fused_computation.25 | convolution fusion | flops 3240099840 | bytes 27525120 | tf_op jit(solution)/shard_map/bctsk,bcskp->bctkp/dot_general | solution.py:35
  487.5 0.5 copy.97
  488.1 0.1 copy-done.7
  488.2 1.7 fusion.26
  489.9 2.2 copy.86
  492.0 1.9 copy.100
  493.9 27.9 %convolution_bitcast_fusion = f32[8192,1024]{0,1:T(8,128)} fusion(bf16[1024,1024]{0,1:T(8,128)(2,1)} %bitcast.145, bf16[1024,8192]{1,0:T(8,128)(2,1)} %param.18), kind=kOutput, calls=%fused_computation.3 | convolution fusion | flops 17179869184 | bytes 52428800 | tf_op jit(solution)/shard_map/dot_general | solution.py:125
  521.9 0.6 copy-done.9
  522.5 0.1 dynamic_slice.3
  522.6 0.1 broadcast_multiply_fusion.1
  522.7 0.1 mul.117
  522.9 3.7 fusion.39
  526.6 0.1 copy.105
  526.7 4.7 all_to_all.30
  531.4 1.1 reduce_sum.22
  532.6 532.5 %reduce-scatter.5.cloned.1.call-done = f32[1024,1024]{0,1:T(8,128)} async-done(((f32[8192,1024]{0,1:T(8,128)}), f32[1024,1024]{0,1:T(8,128)}) %reduce-scatter.5.cloned.1.call-update) | async-done | bytes 4194320 | tf_op jit(solution)/shard_map/reduce_scatter | solution.py:124
  1065.1 3.8 convert_element_type.46
  (34 shorter events, 0.2 us)
Async XLA Ops:
  7.2 287.1 %copy-start = (bf16[4096,128]{1,0:T(8,128)(2,1)S(1)}, bf16[4096,128]{1,0:T(8,128)(2,1)}, u32[]{:S(2)}) copy-start(bf16[4096,128]{1,0:T(8,128)(2,1)} %param.17) | copy-start | bytes 3145732
  7.2 234.6 %all-gather.2.cloned.1.call-start = ((), (), s32[]{:S(2)}) async-start(), calls=%async_computation.5 | async-start | bytes 18874368 | tf_op jit(solution)/shard_map/all_gather | solution.py:85
  11.3 378.0 %reduce-scatter.3.cloned.1.call-start = ((), (), s32[]{:S(2)}) async-start(), calls=%async_computation.6 | async-start | bytes 26935296 | tf_op jit(solution)/shard_map/reduce_scatter | solution.py:89
  363.2 0.7 copy-start.8
  363.2 1.6 copy-start.2
  364.8 9.1 copy-start.4
  367.4 6.3 all-to-all-start.1
  371.2 693.9 %reduce-scatter.5.cloned.1.call-start = ((), (), s32[]{:S(2)}) async-start(), calls=%async_computation.7 | async-start | bytes 37748736 | tf_op jit(solution)/shard_map/reduce_scatter | solution.py:124
  409.6 6.8 slice-start
  409.6 6.9 copy-start.5
  409.6 6.9 copy-start.6
  420.6 20.3 %collective-permute-start = (bf16[1024,128]{0,1:T(8,128)(2,1)S(1)}, bf16[1024,128]{0,1:T(8,128)(2,1)S(1)}, u32[]{:S(2)}, u32[]{:S(2)}) collective-permute-start(bf16[1024,128]{0,1:T(8,128)(2,1)S(1)} %slice.83), channel_id=1, source_target_pairs={{0,2},{2,0},{4,6},{6,4},{8,10},{10,8},{12,14},{14,12},{1,3},{3,1},... | collective-permute-start | bytes 786440 | tf_op jit(solution)/shard_map/ppermute | solution.py:18
  464.5 10.1 copy-start.3
  464.5 23.5 %slice-start.1 = ((s8[4456448]{0:T(1024)(128)(4,1)}), s8[4194304]{0:T(1024)(128)(4,1)S(1)}, s32[]{:S(2)}) async-start(s8[4456448]{0:T(1024)(128)(4,1)} %bitcast.129), calls=%async_computation.9 | async-start | bytes 8388608
  474.6 13.5 %slice-start.2 = ((s8[4456448]{0:T(1024)(128)(4,1)}), s8[262144]{0:T(1024)(128)(4,1)S(1)}, s32[]{:S(2)}) async-start(s8[4456448]{0:T(1024)(128)(4,1)} %bitcast.129), calls=%async_computation.10 | async-start | bytes 524288
  487.5 0.7 copy-start.7
  521.8 0.7 copy-start.9
  526.7 542.2 %copy-start.1 = (bf16[4096,128]{1,0:T(8,128)(2,1)S(1)}, bf16[4096,128]{1,0:T(8,128)(2,1)}, u32[]{:S(2)}) copy-start(bf16[4096,128]{1,0:T(8,128)(2,1)} %param.17) | copy-start | bytes 3145732
Sparse Core Ops, SparseCore 0:
  11.4 230.2 all-gather.1
  363.4 25.9 reduce-scatter.2
  522.0 543.0 reduce-scatter.4
where the time goes:
time: 1080 us
  waiting for transfers between devices  780 us (72%)
  matrix products  133 us (12%)
  local copies, waits for them, and re-layouts  68.7 us (6%)
  other arithmetic  36.6 us (3%)
  blocking collectives  36.2 us (3%)
  between operations  14.5 us (1%)
    reduce_scatter x1, waiting for transfers between devices, body(): lax.psum_scatter(lax.dot_general(out_weight, gated, (((0,), (1,)), ((), (...  533 us
    all_gather x1, waiting for transfers between devices, body(): whole_rows = lax.all_gather(flat_tokens, 'head', axis=1, tiled=True)  230 us
    dot_general x1, matrix products, body(): jnp.dot(half_rows, in_weight, preferred_element_type=jnp.float32)  45.6 us
    all_to_all x1, blocking collectives, body(): lax.all_to_all(whole_rows, 'req', split_axis=1, concat_axis=0, tiled=True)  31.5 us
    dot_general x1, matrix products, body(): lax.dot_general(out_weight, gated, (((0,), (1,)), ((), ())), preferred_el...  27.9 us
  transfers between devices with their start and end apart: 5, of which 4 were waited for; matrix products, arithmetic and copies ran while one was open for 2% of the time, Pallas kernels for 0%

commit v1 on v0

v1 whole, which is shorter than its diff:
```python
import functools
import jax
import jax.numpy as jnp
from jax import lax
from jax.experimental import pallas as pl
from jax.experimental.pallas import tpu as pltpu
from jax.sharding import PartitionSpec as P

P_SIZE = 64
N = 128
G = 4
Q = 256
PAIR = 2 * P_SIZE


def from_partner(value, axis, bit):
    mask = 2**bit
    pairs = [(source, source ^ mask) for source in range(lax.axis_size(axis))]
    return lax.ppermute(value, axis, pairs)


def scan_kernel(
    len_ref, x_ref, gate_ref, b_ref, c_ref, decay_ref, step_ref, row_ref, skip_ref, init_ref,
    out_ref, final_ref, scores_ref,
):
    spans = x_ref.shape[0] // Q
    t_index = lax.broadcasted_iota(jnp.int32, (Q, Q), 0)
    s_index = lax.broadcasted_iota(jnp.int32, (Q, Q), 1)

    @pl.when(pl.program_id(0) == 0)
    def _():
        for k in range(spans):
            rows = pl.ds(k * Q, Q)
            scores = lax.dot_general(
                c_ref[rows, :], b_ref[rows, :], (((1,), (1,)), ((), ())),
                preferred_element_type=jnp.float32,
            )
            scores_ref[k] = jnp.where(t_index >= s_index, scores, 0.0)

    first_lane = lax.broadcasted_iota(jnp.int32, (Q, PAIR), 1) < P_SIZE
    first_row = lax.broadcasted_iota(jnp.int32, (PAIR, N), 0) < P_SIZE
    position = lax.broadcasted_iota(jnp.int32, (Q, PAIR), 0)
    state = init_ref[...].astype(jnp.float32)
    for k in range(spans):
        rows = pl.ds(k * Q, Q)
        x = x_ref[rows, :].astype(jnp.float32)
        decay = decay_ref[rows, :]
        steps = step_ref[rows, :]
        stepped = x * steps
        stepped_cast = stepped.astype(jnp.bfloat16)
        scores = scores_ref[k]
        mixes = []
        for j in range(2):
            spread = decay[:, j * P_SIZE : j * P_SIZE + 1] - row_ref[0, j : j + 1, rows]
            weights = scores * jnp.exp(jnp.minimum(spread, 0.0))
            mixes.append(
                jnp.dot(
                    weights.astype(jnp.bfloat16), stepped_cast,
                    preferred_element_type=jnp.float32,
                )
            )
        intra = jnp.where(first_lane, mixes[0], mixes[1])
        carried = jnp.exp(decay) * lax.dot_general(
            c_ref[rows, :], state.astype(jnp.bfloat16), (((1,), (1,)), ((), ())),
            preferred_element_type=jnp.float32,
        )
        last = decay[Q - 1 : Q, :]
        leaving = (stepped * jnp.exp(last - decay)).astype(jnp.bfloat16)
        update = lax.dot_general(
            leaving, b_ref[rows, :], (((0,), (0,)), ((), ())),
            preferred_element_type=jnp.float32,
        )
        through = jnp.exp(
            jnp.where(first_row, last[:, :1], last[:, P_SIZE : P_SIZE + 1])
        )
        state = through * state + update
        gate = gate_ref[rows, :].astype(jnp.float32)
        value = (intra + carried + skip_ref[...] * x) * (gate * jax.nn.sigmoid(gate))
        live = position + k * Q < len_ref[0]
        out_ref[rows, :] = jnp.where(live, value, 0.0).astype(jnp.bfloat16)
    final_ref[...] = state.astype(jnp.bfloat16)


def scan(length, projected, decay, steps, skip, initial):
    tokens, head_count = steps.shape
    width = head_count * P_SIZE
    pairs = width // PAIR
    by_lane = lambda value: jnp.repeat(value, P_SIZE, axis=1)
    rows = decay.T.reshape(pairs, 2, tokens)
    column = lambda base: pl.BlockSpec((tokens, PAIR), lambda p: (0, base + p))
    fixed = lambda place: pl.BlockSpec((tokens, N), lambda p: (0, place))
    return pl.pallas_call(
        scan_kernel,
        grid=(pairs,),
        out_shape=(
            jax.ShapeDtypeStruct((tokens, width), jnp.bfloat16),
            jax.ShapeDtypeStruct((width, N), jnp.bfloat16),
        ),
        in_specs=[
            pl.BlockSpec(memory_space=pltpu.SMEM),
            column(0),
            column(pairs),
            fixed(2 * pairs),
            fixed(2 * pairs + 1),
            column(0),
            column(0),
            pl.BlockSpec((1, 2, tokens), lambda p: (p, 0, 0)),
            pl.BlockSpec((1, PAIR), lambda p: (0, p)),
            pl.BlockSpec((PAIR, N), lambda p: (p, 0)),
        ],
        out_specs=(column(0), pl.BlockSpec((PAIR, N), lambda p: (p, 0))),
        scratch_shapes=[pltpu.VMEM((tokens // Q, Q, Q), jnp.float32)],
        compiler_params=pltpu.CompilerParams(vmem_limit_bytes=32 * 1024 * 1024),
        cost_estimate=pl.CostEstimate(
            flops=pairs * tokens * 2 * PAIR * (2 * Q + 2 * N),
            bytes_accessed=tokens * width * 16,
            transcendentals=head_count * tokens * Q,
        ),
    )(length, projected, projected, projected, projected, by_lane(decay), by_lane(steps), rows,
      by_lane(skip[None, :]), initial)


def fetch_states(hit_slots, state_pool, local_requests):
    slot_count = state_pool.shape[0]
    local_slot = hit_slots - lax.axis_index("req") * slot_count
    selector = (local_slot[:, None] == jnp.arange(slot_count)[None, :]).astype(jnp.bfloat16)
    outgoing = jnp.dot(
        selector, state_pool.reshape(slot_count, -1), preferred_element_type=jnp.float32
    )
    outgoing = outgoing.astype(jnp.bfloat16).reshape((hit_slots.shape[0],) + state_pool.shape[1:])
    incoming = lax.all_to_all(outgoing, "req", split_axis=0, concat_axis=0, tiled=True)
    incoming = incoming.reshape((lax.axis_size("req"), local_requests) + state_pool.shape[1:])
    return jnp.sum(incoming.astype(jnp.float32), axis=0).astype(jnp.bfloat16)


def arrange_weights(in_weight, group_weight, head_count):
    group_devices = lax.axis_size("head") // G
    place = lax.axis_index("head") % group_devices
    for bit in range(group_devices.bit_length() - 1):
        partner = from_partner(group_weight, "head", bit)
        upper = place // (1 << bit) % 2 == 1
        group_weight = jnp.where(
            upper,
            jnp.concatenate([partner, group_weight], axis=1),
            jnp.concatenate([group_weight, partner], axis=1),
        )
    by_head = in_weight.reshape(in_weight.shape[0], head_count, -1)
    part = lambda low, high: by_head[:, :, low:high].reshape(in_weight.shape[0], -1)
    main = jnp.concatenate(
        [part(0, P_SIZE), part(P_SIZE, 2 * P_SIZE), group_weight], axis=1
    )
    step = part(2 * P_SIZE, 2 * P_SIZE + 1)
    whole = []
    upper = lax.axis_index("req") == 1
    for own in (main, step):
        other = from_partner(own, "req", 0)
        whole.append(
            jnp.where(
                upper,
                jnp.concatenate([other, own], axis=0),
                jnp.concatenate([own, other], axis=0),
            )
        )
    return whole


def body(
    hidden,
    lengths,
    hit_slots,
    placement,
    state_pool,
    in_weight,
    group_weight,
    out_weight,
    decay_rate,
    step_bias,
    skip_gain,
):
    local_requests, length, feature_piece = hidden.shape
    head_count = decay_rate.shape[0]
    rows = [
        lax.all_gather(hidden[r], "head", axis=1, tiled=True) for r in range(local_requests)
    ]
    main_weight, step_weight = arrange_weights(in_weight, group_weight, head_count)
    initial = fetch_states(hit_slots, state_pool, local_requests)
    out_blocks = out_weight.reshape(out_weight.shape[0], -1, feature_piece)
    mixed, finals = [], []
    for r in range(local_requests):
        projected = jnp.dot(rows[r], main_weight, preferred_element_type=jnp.float32)
        projected = projected.astype(jnp.bfloat16)
        step_raw = jnp.dot(rows[r], step_weight, preferred_element_type=jnp.float32)
        live = jnp.arange(length)[:, None] < lengths[r]
        steps = jnp.where(live, jax.nn.softplus(step_raw + step_bias), 0.0)
        decay = jnp.cumsum((-steps * decay_rate).reshape(-1, Q, head_count), axis=1)
        gated, final = scan(
            lengths[r][None],
            projected,
            decay.reshape(length, head_count),
            steps,
            skip_gain,
            initial[r].reshape(head_count * P_SIZE, N),
        )
        finals.append(final)
        partial = jnp.einsum(
            "tk,kjc->jtc", gated, out_blocks, preferred_element_type=jnp.float32
        ).astype(jnp.bfloat16)
        mixed.append(lax.psum_scatter(partial, "head", scatter_dimension=0, tiled=True))
    mixed = jnp.concatenate(mixed, axis=0)
    request_total = placement.shape[0]
    my_targets = lax.dynamic_slice_in_dim(
        placement, lax.axis_index("req") * local_requests, local_requests, 0
    )
    finals = jnp.stack(finals)
    leaving = jnp.zeros((request_total,) + finals.shape[1:], jnp.float32)
    for r in range(local_requests):
        chosen = jnp.arange(request_total)[:, None, None] == my_targets[r]
        leaving = leaving + jnp.where(chosen, finals[r].astype(jnp.float32), 0.0)
    leaving = leaving.astype(jnp.bfloat16)
    arrived = lax.all_to_all(leaving, "req", split_axis=0, concat_axis=0, tiled=True)
    arrived = arrived.reshape(lax.axis_size("req"), local_requests, head_count, P_SIZE, N)
    decode_states = jnp.sum(arrived.astype(jnp.float32), axis=0).astype(jnp.bfloat16)
    return (mixed, decode_states)


def solution(mesh):
    in_specs = (
        P(("rep", "req"), None, "head"),
        P(("rep", "req")),
        P("rep"),
        P("rep"),
        P(("rep", "req"), "head", None, None),
        P("req", "head"),
        P("req", "head"),
        P("head", None),
        P("head"),
        P("head"),
        P("head"),
    )
    out_specs = (P(("rep", "req"), None, "head"), P(("rep", "req"), "head", None, None))
    return jax.shard_map(body, mesh=mesh, in_specs=in_specs, out_specs=out_specs, check_vma=False)
```

time: 1080 us -> 714 us (0.66)
  waiting for transfers between devices: 780 us -> 397 us
  other arithmetic: 36.6 us -> 91.8 us
  matrix products: 133 us -> 103 us
  Pallas kernels: 0 us -> 13.2 us
  local copies, waits for them, and re-layouts: 68.7 us -> 57.7 us
    reduce_scatter x2, waiting for transfers between devices: 548 us -> 230 us  [body(): lax.psum_scatter(partial, 'head', scatter_dimension=0, tiled=True)]
    all_gather x1 -> x2, waiting for transfers between devices: 230 us -> 163 us  [body(): lax.all_gather(hidden[r], 'head', axis=1, tiled=True)]
    select_n x1 -> x2, other arithmetic: 1.15 us -> 66.6 us  [the longest x1 64.5 us: arrange_weights(): jnp.where(upper, jnp.concatenate([other, own], axis=0), jnp.concatenate([...]
    dot_general x8 -> x6, matrix products: 132 us -> 99.8 us  [the longest x2 54.7 us: body(): jnp.dot(rows[r], main_weight, preferred_element_type=jnp.float32)]
    all_to_all x1 -> x0, local copies, waits for them, and re-layouts: 21 us -> none  [body(): lax.all_to_all(whole_rows, 'req', split_axis=1, concat_axis=0, tiled=True)]
    pallas_call x0 -> x2, Pallas kernels: none -> 13.2 us  [scan(): pl.pallas_call(scan_kernel, grid=(pairs,), out_shape=(jax.ShapeDtypeStruc...]
    reshape x6 -> x10, local copies, waits for them, and re-layouts: 29.2 us -> 29 us  [the longest x1 19.3 us: arrange_weights(): by_head = in_weight.reshape(in_weight.shape[0], head_count, -1)]
  transfers between devices with their start and end apart: 5 -> 7, of which waited for: 4 -> 5; matrix products, arithmetic and copies ran while one was open for 2% -> 19% of each run, Pallas kernels for 0% -> 1%
where the time goes in v1:
time: 714 us; the launch traced here: 707 us
  waiting for transfers between devices  397 us (56%)
  matrix products  103 us (14%)
  other arithmetic  91.8 us (13%)
  local copies, waits for them, and re-layouts  57.7 us (8%)
  blocking collectives  27 us (4%)
  between operations  14.5 us (2%)
  Pallas kernels  13.2 us (2%)
    reduce_scatter x2, waiting for transfers between devices, body(): lax.psum_scatter(partial, 'head', scatter_dimension=0, tiled=True)  230 us
    all_gather x2, waiting for transfers between devices, body(): lax.all_gather(hidden[r], 'head', axis=1, tiled=True)  163 us
    select_n x1, other arithmetic, arrange_weights(): jnp.where(upper, jnp.concatenate([other, own], axis=0), jnp.concatenate([...  64.5 us
    dot_general x2, matrix products, body(): jnp.dot(rows[r], main_weight, preferred_element_type=jnp.float32)  54.7 us
    dot_general x2, matrix products, body(): jnp.einsum('tk,kjc->jtc', gated, out_blocks, preferred_element_type=jnp.f...  33.7 us
    all_to_all x1, blocking collectives, fetch_states(): lax.all_to_all(outgoing, 'req', split_axis=0, concat_axis=0, tiled=True)  22.4 us
    reshape x1, local copies, waits for them, and re-layouts, arrange_weights(): by_head = in_weight.reshape(in_weight.shape[0], head_count, -1)  19.3 us
    concatenate x1, other arithmetic, arrange_weights(): jnp.concatenate([part(0, P_SIZE), part(P_SIZE, 2 * P_SIZE), group_weight]...  15 us
  transfers between devices with their start and end apart: 7, of which 5 were waited for; matrix products, arithmetic and copies ran while one was open for 19% of the time, Pallas kernels for 1%

profile of v1, /device:TPU:0, one launch (start us, length us, event | category | flops | bytes accessed | tf_op | source)
XLA Modules:
  0.0 707.4 jit_solution(2918209623443339975)
XLA Ops:
  7.2 0.0 all-gather.7.cloned.1.call-start
  7.2 3.1 fusion.59
  10.3 0.0 all-gather.7.cloned.1.call-update
  10.3 0.0 all-gather.5.cloned.1.call-start
  10.4 3.0 collective-permute-start
  13.4 19.3 %reshape.109 = bf16[4096,16,129]{0,2,1:T(8,128)(2,1)} reshape(bf16[4096,2064]{0,1:T(8,128)(2,1)} %param.16) | data formatting | bytes 33816576 | tf_op jit(solution)/shard_map/reshape | solution.py:147
  32.6 11.9 %fusion.58 = (bf16[4096,16,64]{0,2,1:T(8,128)(2,1)}, bf16[4096,16,64]{0,2,1:T(8,128)(2,1)}) fusion(bf16[4096,16,129]{0,2,1:T(8,128)(2,1)} %reshape.109), kind=kLoop, calls=%fused_computation.62 | loop fusion | bytes 33554432 | tf_op jit(solution)/shard_map/slice | solution.py:148
  44.5 3.5 collective-permute-done
  48.0 2.1 maximum_select_fusion.1
  50.1 2.9 copy.54
  53.0 15.0 %pad_maximum_fusion = bf16[4096,2304]{0,1:T(8,128)(2,1)} fusion(bf16[4096,256]{0,1:T(8,128)(2,1)S(1)} %copy.54, bf16[4096,1024]{0,1:T(8,128)(2,1)} %bitcast.142, bf16[4096,1024]{0,1:T(8,128)(2,1)} %bitcast.140), kind=kLoop, calls=%fused_computation.2 | loop fusion | flops 56623104 | bytes 37748736 | tf_op jit(solution)/shard_map/concatenate | solution.py:149
  68.0 0.1 collective-permute-start.1
  68.1 0.0 all-gather.5.cloned.1.call-update
  68.1 0.0 reduce-scatter.3.cloned.1.call-start
  68.2 1.7 slice.64
  69.9 0.2 copy.112
  70.1 0.6 collective-permute-start.2
  70.7 3.0 fusion.32
  73.7 0.1 copy.84
  73.9 22.4 %all_to_all.10 = bf16[4,16,64,128]{3,2,1,0:T(8,128)(2,1)S(1)} all-to-all(bf16[4,16,64,128]{3,2,1,0:T(8,128)(2,1)S(1)} %bitcast.149), channel_id=1, replica_groups=mesh['rep'=2,'head'=8,'req'=2] {'req'}, dimensions={0} | all-to-all | bytes 2097152 | tf_op jit(solution)/shard_map/all_to_all | solution.py:131
  96.3 0.2 reduce_sum.24
  96.5 0.6 fusion.62
  97.2 0.6 iota_compare_fusion
  97.9 0.1 broadcast_in_dim.74
  97.9 0.1 broadcast_in_dim.75.skip_ref
  98.0 0.7 iota_compare_fusion.2
  98.7 43.6 %all-gather.7.cloned.1.call-done = bf16[1,512,8192]{2,1,0:T(8,128)(2,1)} async-done(((bf16[1,512,1024]{2,1,0:T(8,128)(2,1)}), bf16[1,512,8192]{2,1,0:T(8,128)(2,1)}) %all-gather.7.cloned.1.call-update) | async-done | bytes 8388624 | tf_op jit(solution)/shard_map/all_gather | solution.py:183
  142.3 5.7 fusion.50
  147.9 119.6 %all-gather.5.cloned.1.call-done = bf16[1,512,8192]{2,1,0:T(8,128)(2,1)} async-done(((bf16[1,512,1024]{2,1,0:T(8,128)(2,1)}), bf16[1,512,8192]{2,1,0:T(8,128)(2,1)}) %all-gather.5.cloned.1.call-update) | async-done | bytes 8388624 | tf_op jit(solution)/shard_map/all_gather | solution.py:183
  267.6 5.7 negate_multiply_fusion.1
  273.3 1.2 reduce-window.14
  274.4 0.2 slice_reduce_fusion.1
  274.6 0.1 bitcast_bitcast_fusion.1
  274.7 1.6 broadcast_in_dim.72
  276.3 1.9 copy.60.decay_ref
  278.3 1.6 broadcast_in_dim.73
  279.8 2.9 copy.61.step_ref
  282.7 64.5 %maximum_select_fusion = bf16[8192,2304]{0,1:T(8,128)(2,1)} fusion(bf16[4096,256]{0,1:T(8,128)(2,1)} %copy-done.2, bf16[4096,1024]{0,1:T(8,128)(2,1)} %bitcast.143, bf16[4096,1024]{0,1:T(8,128)(2,1)} %bitcast.141, bf16[4096,2304]{0,1:T(8,128)(2,1)} %collective-permute-done.1, pred[]{:T(512)S(6)} %eq.44), kind=kLoop, calls=%fused_computation.1 | loop fusion | flops 320864256 | bytes 75497472 | tf_op jit(solution)/shard_map/jit(_where)/select_n | solution.py:158
  347.2 27.4 %fusion.27.x_ref.gate_ref.b_ref.c_ref = bf16[512,2304]{1,0:T(8,128)(2,1)S(1)} fusion(bf16[8192,2304]{0,1:T(8,128)(2,1)} %maximum_select_fusion, bf16[1,512,8192]{2,1,0:T(8,128)(2,1)} %all-gather.5.cloned.1.call-done), kind=kOutput, calls=%fused_computation.22 | convolution fusion | flops 19328532480 | bytes 48496640 | tf_op jit(solution)/shard_map/dot_general | solution.py:190
  374.6 6.6 shard_map.122
  381.3 16.8 %convert_bitcast_fusion.1 = bf16[8,512,1024]{2,1,0:T(8,128)(2,1)} fusion(bf16[128,8,8,1024]{3,2,1,0:T(8,128)(2,1)} %bitcast.161, bf16[512,1024]{1,0:T(8,128)(2,1)S(1)} %get-tuple-element.6), kind=kOutput, calls=%fused_computation.18 | convolution fusion | flops 8594128896 | bytes 26214400 | tf_op jit(solution)/shard_map/tk,kjc->jtc/dot_general | solution.py:205
  398.0 0.0 reduce-scatter.3.cloned.1.call-update
  398.0 0.0 reduce-scatter.5.cloned.1.call-start
  398.1 1.4 reduce-window.16
  399.5 0.2 slice_reduce_fusion
  399.7 0.1 bitcast_bitcast_fusion
  399.8 1.6 broadcast_in_dim.77
  401.4 1.9 copy.68.decay_ref
  403.3 1.6 broadcast_in_dim.78
  404.9 2.9 copy.69.step_ref
  407.8 27.3 %fusion.24.x_ref.gate_ref.b_ref.c_ref = bf16[512,2304]{1,0:T(8,128)(2,1)S(1)} fusion(bf16[8192,2304]{0,1:T(8,128)(2,1)} %maximum_select_fusion, bf16[1,512,8192]{2,1,0:T(8,128)(2,1)} %all-gather.7.cloned.1.call-done), kind=kOutput, calls=%fused_computation.21 | convolution fusion | flops 19328532480 | bytes 48496640 | tf_op jit(solution)/shard_map/dot_general | solution.py:190
  435.2 6.6 shard_map.123
  441.8 17.0 %convert_bitcast_fusion = bf16[8,512,1024]{2,1,0:T(8,128)(2,1)} fusion(bf16[128,8,8,1024]{3,2,1,0:T(8,128)(2,1)} %bitcast.162, bf16[512,1024]{1,0:T(8,128)(2,1)S(1)} %get-tuple-element.7), kind=kOutput, calls=%fused_computation.17 | convolution fusion | flops 8594128896 | bytes 26214400 | tf_op jit(solution)/shard_map/tk,kjc->jtc/dot_general | solution.py:205
  458.8 0.0 reduce-scatter.5.cloned.1.call-update
  458.8 0.6 copy-done.9
  459.4 0.1 dynamic_slice.3
  459.5 0.6 fusion.61
  460.1 1.3 iota_compare_fusion.4
  461.5 0.3 add_convert_fusion
  461.8 4.6 all_to_all.11
  466.4 1.1 reduce_sum.25
  467.5 77.8 %reduce-scatter.3.cloned.1.call-done = bf16[1,512,1024]{2,1,0:T(8,128)(2,1)} async-done(((bf16[8,512,1024]{2,1,0:T(8,128)(2,1)}), bf16[1,512,1024]{2,1,0:T(8,128)(2,1)}) %reduce-scatter.3.cloned.1.call-update) | async-done | bytes 1048592 | tf_op jit(solution)/shard_map/reduce_scatter | solution.py:208
  545.4 152.0 %reduce-scatter.5.cloned.1.call-done = bf16[1,512,1024]{2,1,0:T(8,128)(2,1)} async-done(((bf16[8,512,1024]{2,1,0:T(8,128)(2,1)}), bf16[1,512,1024]{2,1,0:T(8,128)(2,1)}) %reduce-scatter.5.cloned.1.call-update) | async-done | bytes 1048592 | tf_op jit(solution)/shard_map/reduce_scatter | solution.py:208
  697.3 3.1 pad_maximum_fusion.1
  (35 shorter events, 0.3 us)
Async XLA Ops:
  7.2 135.1 %all-gather.7.cloned.1.call-start = ((), (), s32[]{:S(2)}) async-start(), calls=%async_computation.7 | async-start | bytes 9437184 | tf_op jit(solution)/shard_map/all_gather | solution.py:183
  10.3 257.3 %all-gather.5.cloned.1.call-start = ((), (), s32[]{:S(2)}) async-start(), calls=%async_computation.6 | async-start | bytes 9437184 | tf_op jit(solution)/shard_map/all_gather | solution.py:183
  10.4 37.6 %collective-permute-start = (bf16[4096,128]{1,0:T(8,128)(2,1)}, bf16[4096,128]{1,0:T(8,128)(2,1)S(1)}, u32[]{:S(2)}, u32[]{:S(2)}) collective-permute-start(bf16[4096,128]{1,0:T(8,128)(2,1)} %param.17), channel_id=1, source_target_pairs={{0,2},{2,0},{4,6},{6,4},{8,10},{10,8},{12,14},{14,12},{1,3},{3,1},... | collective-permute-start | bytes 3145736 | tf_op jit(solution)/shard_map/ppermute | solution.py:19
  32.6 15.4 %copy-start.3 = (bf16[4096,128]{1,0:T(8,128)(2,1)S(1)}, bf16[4096,128]{1,0:T(8,128)(2,1)}, u32[]{:S(2)}) copy-start(bf16[4096,128]{1,0:T(8,128)(2,1)} %param.17) | copy-start | bytes 3145732
  53.0 15.1 %copy-start.2 = (bf16[4096,256]{0,1:T(8,128)(2,1)}, bf16[4096,256]{0,1:T(8,128)(2,1)S(1)}, u32[]{:S(2)}) copy-start(bf16[4096,256]{0,1:T(8,128)(2,1)S(1)} %copy.54) | copy-start | bytes 6291460
  53.0 17.7 %copy-start.8 = (s32[4]{0:T(128)S(1)}, s32[4]{0:T(128)}, u32[]{:S(2)}) copy-start(s32[4]{0:T(128)} %param.13) | copy-start | bytes 52
  68.0 28.5 %copy-start.5 = (s32[2]{0:T(128)S(1)}, s32[2]{0:T(128)}, u32[]{:S(2)}) copy-start(s32[2]{0:T(128)} %param.12) | copy-start | bytes 28
  68.0 29.8 %copy-start.7 = (f32[16]{0:T(128)S(1)}, f32[16]{0:T(128)}, u32[]{:S(2)}) copy-start(f32[16]{0:T(128)} %param.21) | copy-start | bytes 196
  68.0 74.2 %copy-start.4 = (f32[16]{0:T(128)S(1)}, f32[16]{0:T(128)}, u32[]{:S(2)}) copy-start(f32[16]{0:T(128)} %param.20) | copy-start | bytes 196
  68.0 214.7 %collective-permute-start.1 = (bf16[4096,2304]{0,1:T(8,128)(2,1)}, bf16[4096,2304]{0,1:T(8,128)(2,1)}, u32[]{:S(2)}, u32[]{:S(2)}) collective-permute-start(bf16[4096,2304]{0,1:T(8,128)(2,1)} %pad_maximum_fusion), channel_id=1, source_target_pairs={{0,1},{1,0},{2,3},{3,2},{4,5},{5,4},{6,7},{7,6},{8,9},{9,8},{10,11... | collective-permute-start | bytes 56623112 | tf_op jit(solution)/shard_map/ppermute | solution.py:19
  68.1 477.2 %reduce-scatter.3.cloned.1.call-start = ((), (), s32[]{:S(2)}) async-start(), calls=%async_computation.4 | async-start | bytes 9437184 | tf_op jit(solution)/shard_map/reduce_scatter | solution.py:208
  70.1 28.6 %collective-permute-start.2 = (bf16[4096,16]{0,1:T(8,128)(2,1)S(1)}, bf16[4096,16]{0,1:T(8,128)(2,1)S(1)}, u32[]{:S(2)}, u32[]{:S(2)}) collective-permute-start(bf16[4096,16]{0,1:T(8,128)(2,1)S(1)} %bitcast.152), channel_id=1, source_target_pairs={{0,1},{1,0},{2,3},{3,2},{4,5},{5,4},{6,7},{7,6},{8,9},{9,8},{10,11... | collective-permute-start | bytes 393224 | tf_op jit(solution)/shard_map/ppermute | solution.py:19
  73.7 193.9 %copy-start.6 = (f32[16]{0:T(128)S(1)}, f32[16]{0:T(128)}, u32[]{:S(2)}) copy-start(f32[16]{0:T(128)} %param.19) | copy-start | bytes 196
  347.2 27.4 %copy-start = (f32[512,1024]{1,0:T(8,128)S(1)}, f32[512,1024]{1,0:T(8,128)}, u32[]{:S(2)}) copy-start(f32[512,1024]{1,0:T(8,128)} %copy.61.step_ref) | copy-start | bytes 6291460
  398.0 299.3 %reduce-scatter.5.cloned.1.call-start = ((), (), s32[]{:S(2)}) async-start(), calls=%async_computation.5 | async-start | bytes 9437184 | tf_op jit(solution)/shard_map/reduce_scatter | solution.py:208
  407.8 27.3 %copy-start.1 = (f32[512,1024]{1,0:T(8,128)S(1)}, f32[512,1024]{1,0:T(8,128)}, u32[]{:S(2)}) copy-start(f32[512,1024]{1,0:T(8,128)} %copy.69.step_ref) | copy-start | bytes 6291460
  458.8 0.7 copy-start.9
Sparse Core Ops, SparseCore 0:
  10.4 131.7 all-gather.6
  144.4 123.0 all-gather.4
  398.1 147.1 reduce-scatter.2
  549.3 147.9 reduce-scatter.4

commit v2 on v1

--- a/solution.py
+++ b/solution.py
@@ -120,6 +120,135 @@
       by_lane(skip[None, :]), initial)
 
 
+def ring_place(index, n):
+    if n != 8:
+        return index
+    return jnp.where(index % 2 == 0, index // 2, n - 1 - index // 2)
+
+
+def ring_index(place, n):
+    place = lax.rem(place + 2 * n, n)
+    if n != 8:
+        return place
+    return jnp.where(place < n // 2, 2 * place, 2 * (n - 1 - place) + 1)
+
+
+def sum_kernel(n, gated_ref, w_ref, out_ref, w_buf, partial, going, coming, w_sem, send_sem, recv_sem):
+    piece = out_ref.shape[-1]
+    chunk = gated_ref.shape[1] // 2
+    place = ring_place(lax.axis_index("head"), n)
+    ways = (1, -1)
+    barrier = pltpu.get_barrier_semaphore()
+    for way in ways:
+        pl.semaphore_signal(
+            barrier, inc=1, device_id={"head": ring_index(place + way, n)},
+            device_id_type=pl.DeviceIdType.MESH,
+        )
+    pl.semaphore_wait(barrier, 2)
+
+    def load(step, slot, d):
+        block = ring_index(place - ways[d] * (step + 1), n)
+        columns = pl.ds(pl.multiple_of(block * piece, piece), piece)
+        return pltpu.make_async_copy(
+            w_ref.at[:, columns], w_buf.at[slot, d], w_sem.at[slot, d]
+        )
+
+    def send(step, d, c):
+        rows = pl.ds(c * chunk, chunk)
+        return pltpu.make_async_remote_copy(
+            src_ref=going.at[step, d, rows],
+            dst_ref=coming.at[step, d, rows],
+            send_sem=send_sem.at[step, d, c],
+            recv_sem=recv_sem.at[step, d, c],
+            device_id={"head": ring_index(place + ways[d], n)},
+            device_id_type=pl.DeviceIdType.MESH,
+        )
+
+    for d in range(2):
+        load(0, 0, d).start()
+
+    def one_step(step, carry):
+        slot = lax.rem(step, 2)
+
+        @pl.when(step < n - 1)
+        def _():
+            for d in range(2):
+                load(step + 1, 1 - slot, d).start()
+
+        for d in range(2):
+            load(step, slot, d).wait()
+        for c in range(2):
+            rows = pl.ds(c * chunk, chunk)
+            for d in range(2):
+                partial[d, rows, :] = jnp.dot(
+                    gated_ref[d, rows, :], w_buf[slot, d], preferred_element_type=jnp.float32
+                )
+        for c in range(2):
+            rows = pl.ds(c * chunk, chunk)
+            for d in range(2):
+
+                @pl.when(step == 0)
+                def _():
+                    going[0, d, rows, :] = partial[d, rows, :].astype(jnp.bfloat16)
+                    send(0, d, c).start()
+
+                @pl.when(jnp.logical_and(step > 0, step < n - 1))
+                def _():
+                    send(step - 1, d, c).wait_recv()
+                    going[step, d, rows, :] = (
+                        partial[d, rows, :] + coming[step - 1, d, rows, :].astype(jnp.float32)
+                    ).astype(jnp.bfloat16)
+                    send(step, d, c).start()
+
+                @pl.when(step == n - 1)
+                def _():
+                    send(n - 2, d, c).wait_recv()
+                    out_ref[d, rows, :] = (
+                        partial[d, rows, :] + coming[n - 2, d, rows, :].astype(jnp.float32)
+                    ).astype(jnp.bfloat16)
+
+        return carry
+
+    lax.fori_loop(0, n, one_step, 0)
+
+    def drain(step, carry):
+        for d in range(2):
+            for c in range(2):
+                send(step, d, c).wait_send()
+        return carry
+
+    lax.fori_loop(0, n - 1, drain, 0)
+
+
+def output_sum(gated, out_weight, piece):
+    n = lax.axis_size("head")
+    requests, tokens, depth = gated.shape
+    slots = (n - 1, requests, tokens, piece)
+    return pl.pallas_call(
+        functools.partial(sum_kernel, n),
+        out_shape=jax.ShapeDtypeStruct((requests, tokens, piece), jnp.bfloat16),
+        in_specs=[pl.BlockSpec(memory_space=pltpu.VMEM), pl.BlockSpec(memory_space=pl.ANY)],
+        out_specs=pl.BlockSpec(memory_space=pltpu.VMEM),
+        scratch_shapes=[
+            pltpu.VMEM((2, 2, depth, piece), jnp.bfloat16),
+            pltpu.VMEM((requests, tokens, piece), jnp.float32),
+            pltpu.VMEM(slots, jnp.bfloat16),
+            pltpu.VMEM(slots, jnp.bfloat16),
+            pltpu.SemaphoreType.DMA((2, 2)),
+            pltpu.SemaphoreType.DMA((n - 1, 2, 2)),
+            pltpu.SemaphoreType.DMA((n - 1, 2, 2)),
+        ],
+        compiler_params=pltpu.CompilerParams(
+            collective_id=0, has_side_effects=True, vmem_limit_bytes=54 * 1024 * 1024
+        ),
+        cost_estimate=pl.CostEstimate(
+            flops=2 * requests * tokens * depth * piece * n,
+            bytes_accessed=depth * piece * n * 2 + requests * tokens * piece * n * 16,
+            transcendentals=0,
+        ),
+    )(gated, out_weight)
+
+
 def fetch_states(hit_slots, state_pool, local_requests):
     slot_count = state_pool.shape[0]
     local_slot = hit_slots - lax.axis_index("req") * slot_count
@@ -151,16 +280,14 @@
     )
     step = part(2 * P_SIZE, 2 * P_SIZE + 1)
     whole = []
-    upper = lax.axis_index("req") == 1
+    mine = lax.axis_index("req")
     for own in (main, step):
+        depth, columns = own.shape
         other = from_partner(own, "req", 0)
-        whole.append(
-            jnp.where(
-                upper,
-                jnp.concatenate([other, own], axis=0),
-                jnp.concatenate([own, other], axis=0),
-            )
-        )
+        both = jnp.zeros((2, depth, columns), own.dtype)
+        both = lax.dynamic_update_slice(both, own[None], (mine, 0, 0))
+        both = lax.dynamic_update_slice(both, other[None], (1 - mine, 0, 0))
+        whole.append(both.reshape(2 * depth, columns))
     return whole
 
 
@@ -179,13 +306,15 @@
 ):
     local_requests, length, feature_piece = hidden.shape
     head_count = decay_rate.shape[0]
-    rows = [
-        lax.all_gather(hidden[r], "head", axis=1, tiled=True) for r in range(local_requests)
-    ]
+    rows = [lax.all_gather(hidden[0], "head", axis=1, tiled=True)]
     main_weight, step_weight = arrange_weights(in_weight, group_weight, head_count)
+    for r in range(1, local_requests):
+        later, main_weight, step_weight = lax.optimization_barrier(
+            (hidden[r], main_weight, step_weight)
+        )
+        rows.append(lax.all_gather(later, "head", axis=1, tiled=True))
     initial = fetch_states(hit_slots, state_pool, local_requests)
-    out_blocks = out_weight.reshape(out_weight.shape[0], -1, feature_piece)
-    mixed, finals = [], []
+    gated_all, finals = [], []
     for r in range(local_requests):
         projected = jnp.dot(rows[r], main_weight, preferred_element_type=jnp.float32)
         projected = projected.astype(jnp.bfloat16)
@@ -202,11 +331,8 @@
             initial[r].reshape(head_count * P_SIZE, N),
         )
         finals.append(final)
-        partial = jnp.einsum(
-            "tk,kjc->jtc", gated, out_blocks, preferred_element_type=jnp.float32
-        ).astype(jnp.bfloat16)
-        mixed.append(lax.psum_scatter(partial, "head", scatter_dimension=0, tiled=True))
-    mixed = jnp.concatenate(mixed, axis=0)
+        gated_all.append(gated)
+    mixed = output_sum(jnp.stack(gated_all), out_weight, feature_piece)
     request_total = placement.shape[0]
     my_targets = lax.dynamic_slice_in_dim(
         placement, lax.axis_index("req") * local_requests, local_requests, 0

time: 714 us -> 600 us (0.84)
  waiting for transfers between devices: 397 us -> 162 us
  Pallas kernels: 13.2 us -> 182 us
  local copies, waits for them, and re-layouts: 57.7 us -> 121 us
  other arithmetic: 91.8 us -> 43.7 us
  matrix products: 103 us -> 63.8 us
  blocking collectives: 27 us -> 4.58 us
    reduce_scatter x2 -> x0, waiting for transfers between devices: 230 us -> none  [body(): lax.psum_scatter(partial, 'head', scatter_dimension=0, tiled=True)]
    pallas_call x0 -> x1, Pallas kernels: none -> 168 us  [output_sum(): pl.pallas_call(functools.partial(sum_kernel, n), out_shape=jax.ShapeDtype...]
    select_n x1 -> x0, other arithmetic: 64.5 us -> none  [arrange_weights(): jnp.where(upper, jnp.concatenate([other, own], axis=0), jnp.concatenate([...]
    dot_general x2 -> x0, matrix products: 33.7 us -> none  [body(): jnp.einsum('tk,kjc->jtc', gated, out_blocks, preferred_element_type=jnp.f...]
    all_gather x2, waiting for transfers between devices: 163 us -> 139 us  [the longest x1 98.1 us: body(): rows.append(lax.all_gather(later, 'head', axis=1, tiled=True))]
    reshape x1 -> x3, local copies, waits for them, and re-layouts: 0.01 us -> 24 us  [the longest x2 24 us: arrange_weights(): by_head[:, :, low:high].reshape(in_weight.shape[0], -1)]
    all_to_all x1 -> x0, blocking collectives: 22.4 us -> none  [fetch_states(): lax.all_to_all(outgoing, 'req', split_axis=0, concat_axis=0, tiled=True)]
    dynamic_update_slice x0 -> x3, local copies, waits for them, and re-layouts: none -> 20.2 us  [the longest x2 18.5 us: arrange_weights(): both = lax.dynamic_update_slice(both, other[None], (1 - mine, 0, 0))]
  transfers between devices with their start and end apart: 7 -> 6, of which waited for: 5 -> 4; matrix products, arithmetic and copies ran while one was open for 19% -> 24% of each run, Pallas kernels for 1% -> 0%
where the time goes in v2:
time: 600 us; the launch traced here: 598 us
  Pallas kernels  182 us (30%)
  waiting for transfers between devices  162 us (27%)
  local copies, waits for them, and re-layouts  121 us (20%)
  matrix products  63.8 us (11%)
  other arithmetic  43.7 us (7%)
  between operations  14.4 us (2%)
  starting transfers between devices  7.26 us (1%)
    pallas_call x1, Pallas kernels, output_sum(): pl.pallas_call(functools.partial(sum_kernel, n), out_shape=jax.ShapeDtype...  168 us
    all_gather x1, waiting for transfers between devices, body(): rows.append(lax.all_gather(later, 'head', axis=1, tiled=True))  98.1 us
    dot_general x2, matrix products, body(): jnp.dot(rows[r], main_weight, preferred_element_type=jnp.float32)  54.2 us
    all_gather x1, waiting for transfers between devices, body(): rows = [lax.all_gather(hidden[0], 'head', axis=1, tiled=True)]  40.7 us
    reshape x2, local copies, waits for them, and re-layouts, arrange_weights(): by_head[:, :, low:high].reshape(in_weight.shape[0], -1)  24 us
    ppermute x3, waiting for transfers between devices, from_partner(): return lax.ppermute(value, axis, pairs)  20.9 us
    reshape x1, local copies, waits for them, and re-layouts, arrange_weights(): by_head = in_weight.reshape(in_weight.shape[0], head_count, -1)  18.7 us
    dynamic_update_slice x2, local copies, waits for them, and re-layouts, arrange_weights(): both = lax.dynamic_update_slice(both, other[None], (1 - mine, 0, 0))  18.5 us
  transfers between devices with their start and end apart: 6, of which 4 were waited for; matrix products, arithmetic and copies ran while one was open for 24% of the time, Pallas kernels for 0%

profile of v2, /device:TPU:0, one launch (start us, length us, event | category | flops | bytes accessed | tf_op | source)
XLA Modules:
  0.0 598.0 jit_solution(6677524965598159532)
XLA Ops:
  7.2 3.0 collective-permute-start
  10.2 18.7 %reshape.112 = bf16[4096,16,129]{0,2,1:T(8,128)(2,1)} reshape(bf16[4096,2064]{0,1:T(8,128)(2,1)} %param.16) | data formatting | bytes 33816576 | tf_op jit(solution)/shard_map/reshape | solution.py:276
  29.0 11.8 %fusion.27 = (bf16[4096,16,64]{0,2,1:T(8,128)(2,1)}, bf16[4096,16,64]{0,2,1:T(8,128)(2,1)}) fusion(bf16[4096,16,129]{0,2,1:T(8,128)(2,1)} %reshape.112), kind=kLoop, calls=%fused_computation.47 | loop fusion | bytes 33554432 | tf_op jit(solution)/shard_map/slice | solution.py:277
  40.7 12.0 %copy.51 = bf16[4096,1024]{1,0:T(8,128)(2,1)} copy(bf16[4096,1024]{0,1:T(8,128)(2,1)} %bitcast.124) | data formatting | bytes 16777216 | tf_op jit(solution)/shard_map/reshape | solution.py:277
  52.7 12.0 %copy.52 = bf16[4096,1024]{1,0:T(8,128)(2,1)} copy(bf16[4096,1024]{0,1:T(8,128)(2,1)} %bitcast.123) | data formatting | bytes 16777216 | tf_op jit(solution)/shard_map/reshape | solution.py:277
  64.8 2.2 maximum_select_fusion
  66.9 15.5 %pad_maximum_fusion = bf16[4096,2304]{1,0:T(8,128)(2,1)} fusion(bf16[4096,256]{1,0:T(8,128)(2,1)S(1)} %maximum_select_fusion, bf16[4096,1024]{1,0:T(8,128)(2,1)} %copy.52, bf16[4096,1024]{1,0:T(8,128)(2,1)} %copy.51), kind=kLoop, calls=%fused_computation.1 | loop fusion | flops 56623104 | bytes 37748736 | tf_op jit(solution)/shard_map/concatenate | solution.py:278
  82.5 3.0 fusion.28
  85.6 1.7 fusion.26
  87.3 0.2 copy.96
  87.5 0.6 collective-permute-start.2
  88.0 0.2 broadcast_in_dim.89
  88.2 1.7 dynamic_update_slice.14
  89.9 20.9 %collective-permute-done.2 = bf16[4096,16]{0,1:T(8,128)(2,1)S(1)} collective-permute-done((bf16[4096,16]{0,1:T(8,128)(2,1)S(1)}, bf16[4096,16]{0,1:T(8,128)(2,1)S(1)}, u32[]{:S(2)}, u32[]{:S(2)}) %collective-permute-start.2) | collective-permute-done | bytes 131104 | tf_op jit(solution)/shard_map/ppermute | solution.py:19
  110.8 0.2 copy.54
  111.1 1.7 dynamic_update_slice.15
  112.8 0.2 copy.78
  112.9 12.4 %broadcast_in_dim.86 = bf16[2,4096,2304]{2,1,0:T(8,128)(2,1)} broadcast(bf16[]{:T(256)} %constant.47.clone.1), dimensions={} | broadcast | bytes 37748736 | tf_op jit(solution)/shard_map/broadcast_in_dim | solution.py:287
  125.3 15.6 %bitcast_dynamic-update-slice_fusion.1 = bf16[2,4096,2304]{2,1,0:T(8,128)(2,1)} fusion(bf16[2,4096,2304]{2,1,0:T(8,128)(2,1)} %broadcast_in_dim.86, s32[]{:T(128)S(6)} %select_n.57, bf16[4096,256]{1,0:T(8,128)(2,1)S(1)} %maximum_select_fusion, bf16[4096,1024]{1,0:T(8,128)(2,1)} %copy.52, bf16[4096,1024]{1,0:T(8,128)(2,1)} %copy.51), kind=kLoop, calls=%fused_computation.3 | loop fusion | flops 56623104 | bytes 37748740 | tf_op jit(solution)/shard_map/dynamic_update_slice | solution.py:288
  141.0 16.8 %bitcast_dynamic-update-slice_fusion = bf16[2,4096,2304]{2,1,0:T(8,128)(2,1)} fusion(bf16[2,4096,2304]{2,1,0:T(8,128)(2,1)} %bitcast_dynamic-update-slice_fusion.1, s32[]{:T(128)S(6)} %select_n.58, bf16[4096,2304]{1,0:T(8,128)(2,1)} %collective-permute-done.1), kind=kLoop, calls=%fused_computation.2 | loop fusion | bytes 37748740 | tf_op jit(solution)/shard_map/dynamic_update_slice | solution.py:289
  157.8 1.4 fusion.12
  159.3 1.1 copy.80
  160.4 3.6 all-to-all-start
  164.0 2.1 all-to-all-done
  166.1 0.2 reduce_sum.24
  166.4 0.1 broadcast_in_dim.95.skip_ref
  166.6 0.6 fusion.31
  167.2 0.6 iota_compare_fusion
  167.8 0.7 iota_compare_fusion.2
  168.5 0.6 fusion.30
  169.1 1.3 iota_compare_fusion.4
  170.4 40.7 %all-gather.6.cloned.1.call-done = bf16[1,512,8192]{2,1,0:T(8,128)(2,1)} async-done(((bf16[1,512,1024]{2,1,0:T(8,128)(2,1)}), bf16[1,512,8192]{2,1,0:T(8,128)(2,1)}) %all-gather.6.cloned.1.call-update) | async-done | bytes 8388624 | tf_op jit(solution)/shard_map/all_gather | solution.py:309
  211.1 27.1 %fusion.7.x_ref.gate_ref.b_ref.c_ref = bf16[512,2304]{1,0:T(8,128)(2,1)S(1)} fusion(bf16[8192,2304]{1,0:T(8,128)(2,1)} %bitcast.121, bf16[1,512,8192]{2,1,0:T(8,128)(2,1)} %all-gather.6.cloned.1.call-done), kind=kOutput, calls=%fused_computation.10 | convolution fusion | flops 19328532480 | bytes 48496640 | tf_op jit(solution)/shard_map/dot_general | solution.py:319
  238.2 98.1 %all-gather.4.cloned.1.call-done = bf16[512,8192]{1,0:T(8,128)(2,1)} async-done(((bf16[512,1024]{1,0:T(8,128)(2,1)}), bf16[512,8192]{1,0:T(8,128)(2,1)}) %all-gather.4.cloned.1.call-update) | async-done | bytes 8388624 | tf_op jit(solution)/shard_map/all_gather | solution.py:315
  336.3 5.8 fusion.22
  342.2 2.3 negate_multiply_fusion.1
  344.5 1.2 reduce-window.14
  345.7 0.2 slice_reduce_fusion.1
  345.9 0.1 bitcast_bitcast_fusion.1
  346.0 1.6 broadcast_in_dim.92
  347.5 2.9 copy.60.decay_ref
  350.5 1.6 broadcast_in_dim.93
  352.1 2.9 copy.61.step_ref
  355.0 1.6 copy-done.1
  356.6 1.6 copy-done.2
  358.1 6.6 %shard_map.122 = (bf16[512,1024]{1,0:T(8,128)(2,1)S(1)}, bf16[1024,128]{1,0:T(8,128)(2,1)S(1)}) custom-call(s32[1]{0:T(128)} %get-tuple-element.28.len_ref, bf16[512,2304]{1,0:T(8,128)(2,1)S(1)} %fusion.7.x_ref.gate_ref.b_ref.c_ref, bf16[512,2304]{1,0:T(8,128)(2,1)S(1)} %fusion.7.x_ref.gate_ref.b_ref.c_ref, ...), custom_call_target="tpu_custom_call" | custom-call | flops 805306368 | bytes 8388608 | tf_op jit(solution)/shard_map/pallas_call | solution.py:92
  364.8 1.0 copy-done.3
  365.8 0.8 convert_element_type.29
  366.6 1.1 reduce-window.16
  367.7 0.2 slice_reduce_fusion
  367.9 0.1 bitcast_bitcast_fusion
  368.0 1.6 broadcast_in_dim.97
  369.6 1.9 copy.66.decay_ref
  371.5 1.6 broadcast_in_dim.98
  373.1 2.9 copy.67.step_ref
  376.1 27.1 %convolution_convert_fusion.1.x_ref.gate_ref.b_ref.c_ref = bf16[512,2304]{1,0:T(8,128)(2,1)S(1)} fusion(bf16[512,8192]{1,0:T(8,128)(2,1)} %all-gather.4.cloned.1.call-done, bf16[8192,2304]{1,0:T(8,128)(2,1)} %bitcast.122), kind=kOutput, calls=%fused_computation.9 | convolution fusion | flops 19328532480 | bytes 48496640 | tf_op jit(solution)/shard_map/dot_general | solution.py:319
  403.2 6.7 %shard_map.123 = (bf16[512,1024]{1,0:T(8,128)(2,1)S(1)}, bf16[1024,128]{1,0:T(8,128)(2,1)S(1)}) custom-call(s32[1]{0:T(128)} %get-tuple-element.29.len_ref, bf16[512,2304]{1,0:T(8,128)(2,1)S(1)} %convolution_convert_fusion.1.x_ref.gate_ref.b_ref.c_ref, bf16[512,2304]{1,0:T(8,128)(2,1)S(1)} %convolution_convert_fusion.1.x_ref.gate_ref.b_ref.c_ref, ...), custom_call_target="tpu_custom_call" | custom-call | flops 805306368 | bytes 8388608 | tf_op jit(solution)/shard_map/pallas_call | solution.py:92
  410.0 1.0 copy-done.5
  411.0 0.3 add_convert_fusion
  411.3 4.6 all_to_all.10
  415.9 1.1 reduce_sum.25
  417.0 2.7 pad_maximum_fusion.1.gated_ref
  419.8 168.3 %shard_map.124 = bf16[2,512,1024]{2,1,0:T(8,128)(2,1)} custom-call(bf16[2,512,1024]{2,1,0:T(8,128)(2,1)} %pad_maximum_fusion.1.gated_ref, bf16[1024,8192]{1,0:T(8,128)(2,1)} %w_ref.1), custom_call_target="tpu_custom_call" | custom-call | flops 17179869184 | bytes 150994944 | tf_op jit(solution)/shard_map/pallas_call | solution.py:227
  588.1 3.1 copy.102
  (50 shorter events, 0.6 us)
Async XLA Ops:
  7.2 203.9 %all-gather.6.cloned.1.call-start = ((), (), s32[]{:S(2)}) async-start(), calls=%async_computation.3 | async-start | bytes 9437184 | tf_op jit(solution)/shard_map/all_gather | solution.py:309
  7.2 57.6 %collective-permute-start = (bf16[4096,128]{1,0:T(8,128)(2,1)}, bf16[4096,128]{1,0:T(8,128)(2,1)}, u32[]{:S(2)}, u32[]{:S(2)}) collective-permute-start(bf16[4096,128]{1,0:T(8,128)(2,1)} %param.17), channel_id=1, source_target_pairs={{0,2},{2,0},{4,6},{6,4},{8,10},{10,8},{12,14},{14,12},{1,3},{3,1},... | collective-permute-start | bytes 3145736 | tf_op jit(solution)/shard_map/ppermute | solution.py:19
  52.7 12.1 %copy-start.9 = (bf16[4096,128]{1,0:T(8,128)(2,1)S(1)}, bf16[4096,128]{1,0:T(8,128)(2,1)}, u32[]{:S(2)}) copy-start(bf16[4096,128]{1,0:T(8,128)(2,1)} %param.17) | copy-start | bytes 3145732
  82.5 58.5 %collective-permute-start.1 = (bf16[4096,2304]{1,0:T(8,128)(2,1)}, bf16[4096,2304]{1,0:T(8,128)(2,1)}, u32[]{:S(2)}, u32[]{:S(2)}) collective-permute-start(bf16[4096,2304]{1,0:T(8,128)(2,1)} %pad_maximum_fusion), channel_id=1, source_target_pairs={{0,1},{1,0},{2,3},{3,2},{4,5},{5,4},{6,7},{7,6},{8,9},{9,8},{10,11... | collective-permute-start | bytes 56623112 | tf_op jit(solution)/shard_map/ppermute | solution.py:19
  85.5 250.8 %all-gather.4.cloned.1.call-start = ((), (), s32[]{:S(2)}) async-start(), calls=%async_computation.2 | async-start | bytes 9437184 | tf_op jit(solution)/shard_map/all_gather | solution.py:315
  87.5 23.4 %collective-permute-start.2 = (bf16[4096,16]{0,1:T(8,128)(2,1)S(1)}, bf16[4096,16]{0,1:T(8,128)(2,1)S(1)}, u32[]{:S(2)}, u32[]{:S(2)}) collective-permute-start(bf16[4096,16]{0,1:T(8,128)(2,1)S(1)} %bitcast.141), channel_id=1, source_target_pairs={{0,1},{1,0},{2,3},{3,2},{4,5},{5,4},{6,7},{7,6},{8,9},{9,8},{10,11... | collective-permute-start | bytes 393224 | tf_op jit(solution)/shard_map/ppermute | solution.py:19
  141.0 16.8 %copy-start.14 = (s32[4]{0:T(128)S(1)}, s32[4]{0:T(128)}, u32[]{:S(2)}) copy-start(s32[4]{0:T(128)} %param.13) | copy-start | bytes 52
  141.0 16.8 %copy-start.7 = (bf16[8,16,64,128]{3,2,1,0:T(8,128)(2,1)S(1)}, bf16[8,16,64,128]{3,2,1,0:T(8,128)(2,1)}, u32[]{:S(2)}) copy-start(bf16[8,16,64,128]{3,2,1,0:T(8,128)(2,1)} %param.15) | copy-start | bytes 6291460
  157.8 8.6 %copy-start.13 = (f32[16]{0:T(128)S(1)}, f32[16]{0:T(128)}, u32[]{:S(2)}) copy-start(f32[16]{0:T(128)} %param.21) | copy-start | bytes 196
  157.8 8.7 %copy-start.15 = (s32[4]{0:T(128)S(1)}, s32[4]{0:T(128)}, u32[]{:S(2)}) copy-start(s32[4]{0:T(128)} %param.14) | copy-start | bytes 52
  157.8 8.8 %copy-start.11 = (s32[2]{0:T(128)S(1)}, s32[2]{0:T(128)}, u32[]{:S(2)}) copy-start(s32[2]{0:T(128)} %param.12) | copy-start | bytes 28
  160.4 5.7 all-to-all-start
  170.4 165.9 %copy-start.10 = (f32[16]{0:T(128)S(1)}, f32[16]{0:T(128)}, u32[]{:S(2)}) copy-start(f32[16]{0:T(128)} %param.20) | copy-start | bytes 196
  238.2 104.0 %copy-start.12 = (f32[16]{0:T(128)S(1)}, f32[16]{0:T(128)}, u32[]{:S(2)}) copy-start(f32[16]{0:T(128)} %param.19) | copy-start | bytes 196
  336.3 5.8 copy-start.6
  355.0 1.6 copy-start.1
  356.6 1.6 copy-start.2
  364.8 1.0 copy-start.3
  376.1 27.1 %copy-start = (f32[512,1024]{1,0:T(8,128)S(1)}, f32[512,1024]{1,0:T(8,128)}, u32[]{:S(2)}) copy-start(f32[512,1024]{1,0:T(8,128)} %copy.67.step_ref) | copy-start | bytes 6291460
  403.2 7.8 %copy-start.8 = (f32[1024,128]{1,0:T(8,128)S(1)}, f32[1024,128]{1,0:T(8,128)}, u32[]{:S(2)}) copy-start(f32[1024,128]{1,0:T(8,128)} %convert_element_type.29) | copy-start | bytes 1572868
  403.2 13.8 %copy-start.4 = (bf16[512,1024]{1,0:T(8,128)(2,1)S(1)}, bf16[512,1024]{1,0:T(8,128)(2,1)}, u32[]{:S(2)}) copy-start(bf16[512,1024]{1,0:T(8,128)(2,1)} %copy-done.3) | copy-start | bytes 3145732
  410.0 1.0 copy-start.5
Sparse Core Ops, SparseCore 0:
  85.7 125.3 all-gather.5
  213.2 123.0 all-gather.3
